TPU v7x, 128 devices: a whole 4x4x4 slice. The times are simulated.
128 devices in a mesh: seq: 16 (over x, y), head: 8 (over z, core).
Axes of the slice: x: 4, y: 4, z: 4, core: 2. Of those that a mesh axis runs over, the one named last changes fastest.
Arguments:
- query: bfloat16 [4096, 4096], P('seq', 'head'), may hold values from -6 to 6
- key: bfloat16 [4096, 4096], P('seq', 'head'), may hold values from -6 to 6
- value: bfloat16 [4096, 4096], P('seq', 'head'), may hold values from -6 to 6
- head_gain: float32 [4096], P('head'), may hold values from 0.1 to 1.9
- out_weight: bfloat16 [4096, 4096], P('head', 'seq'), may hold values from -0.09375 to 0.09375
- stream: bfloat16 [4096, 4096], P(('seq', 'head')), may hold values from -6 to 6
- model_gain: float32 [4096], replicated, may hold values from 0.1 to 1.9
- expert_ids: int32 [4096, 8], P(('seq', 'head')), may hold values from 0 to 127, all different within a row; in each aligned block of 32 rows (0 to 31, 32 to 63, ...) at most 3 rows name the same one
- expert_gates: float32 [4096, 8], P(('seq', 'head')), may hold values from 0.1 to 0.5
- gate_weight: bfloat16 [128, 4096, 768], P(('seq', 'head')), may hold values from -0.09375 to 0.09375
- up_weight: bfloat16 [128, 4096, 768], P(('seq', 'head')), may hold values from -0.09375 to 0.09375
- down_weight: bfloat16 [128, 768, 4096], P(('seq', 'head')), may hold values from -0.21875 to 0.21875
- weight_scales: float32 [128, 3], P(('seq', 'head')), may hold values from 0.6 to 1.6
Outputs:
- layer_out: bfloat16 [4096, 4096], P(('seq', 'head'))
Inputs may be any that keep to these rules, and one draw needn't show every extreme that they name: `expert_ids`: among the 32 tokens of one device (aligned blocks of rows), no expert is named more than 3 times, a bound that some block reaches; the entries of one row differ.
All inputs are finite; a program needn't handle non-finite values.
Results may differ from a plain program's by a relative error of at most 0.013.
Values may be sent and summed in bfloat16 or wider, within the bound.
No kernel may reach another device: no remote copies, remote signals or barrier semaphores. Data moves between devices by JAX's collectives and lax.ppermute only.
A program may use at most 128 MiB of HBM per device.

v0:
```python
import jax
import jax.numpy as jnp
from jax import lax
from jax.sharding import PartitionSpec as P

D = 4096
HD = 128
TOPK = 8
CAP = 3
NX, NY, NZ, NC = (4, 4, 4, 2)
BF = jnp.bfloat16
F32 = jnp.float32


def shift_x(a, d):
    pairs = [(x * NY + y, (x + d) % NX * NY + y) for x in range(NX) for y in range(NY)]
    return lax.ppermute(a, "seq", pairs)


def shift_y(a, d):
    pairs = [(x * NY + y, x * NY + (y + d) % NY) for x in range(NX) for y in range(NY)]
    return lax.ppermute(a, "seq", pairs)


def shift_z(a, d):
    pairs = [(z * NC + c, (z + d) % NZ * NC + c) for z in range(NZ) for c in range(NC)]
    return lax.ppermute(a, "head", pairs)


def swap_core(a):
    pairs = [(z * NC + c, z * NC + 1 - c) for z in range(NZ) for c in range(NC)]
    return lax.ppermute(a, "head", pairs)


def earlier_states(block_state, x, y):
    own = block_state.astype(BF)
    total = block_state
    before = jnp.zeros_like(block_state)
    for d in range(1, NY):
        got = shift_y(own, d).astype(F32)
        total = total + got
        before = before + jnp.where(y >= d, got, 0.0)
    total = total.astype(BF)
    for d in range(1, NX):
        before = before + jnp.where(x >= d, shift_x(total, d).astype(F32), 0.0)
    return before


def sum_heads(partial, z, c):
    rows = partial.reshape(NZ, NC, -1, partial.shape[-1])
    first = c == 0
    keep = jnp.where(first, rows[:, 0], rows[:, 1])
    give = jnp.where(first, rows[:, 1], rows[:, 0]).astype(BF)
    pair = keep + swap_core(give).astype(F32)
    total = lax.dynamic_index_in_dim(pair, z, 0, False)
    low = pair.astype(BF)
    for d in range(1, NZ):
        total = total + shift_z(lax.dynamic_index_in_dim(low, (z + d) % NZ, 0, False), d).astype(
            F32
        )
    return total


def body(
    query,
    key,
    value,
    head_gain,
    out_weight,
    stream,
    model_gain,
    expert_ids,
    expert_gates,
    gate_weight,
    up_weight,
    down_weight,
    weight_scales,
):
    seq = lax.axis_index("seq")
    head = lax.axis_index("head")
    x, y, z, c = (seq // NY, seq % NY, head // NC, head % NC)
    seq_rows = query.shape[0]
    tok_rows = stream.shape[0]
    heads_local = head_gain.shape[0] // HD
    experts = lax.axis_size("seq") * lax.axis_size("head")
    slots = experts * CAP
    full_out = lax.all_gather(out_weight, "seq", axis=1, tiled=True)
    query_rows = query.reshape(seq_rows, heads_local, HD)
    key_rows = key.reshape(seq_rows, heads_local, HD)
    value_rows = value.reshape(seq_rows, heads_local, HD)
    block_state = jnp.einsum("shd,she->hde", key_rows, value_rows, preferred_element_type=F32)
    prior_state = earlier_states(block_state, x, y)
    scores = jnp.einsum("thd,shd->hts", query_rows, key_rows, preferred_element_type=F32)
    causal = jnp.tril(jnp.ones((seq_rows, seq_rows), dtype=bool))
    scores = jnp.where(causal[None, :, :], scores, 0.0).astype(BF)
    local_part = jnp.einsum("hts,shd->thd", scores, value_rows, preferred_element_type=F32)
    earlier_part = jnp.einsum(
        "thd,hde->the", query_rows, prior_state.astype(BF), preferred_element_type=F32
    )
    mixed_heads = local_part + earlier_part
    mean_square = jnp.mean(mixed_heads * mixed_heads, axis=-1, keepdims=True)
    head_normed = (
        mixed_heads * lax.rsqrt(mean_square + 1e-06) * head_gain.reshape(heads_local, HD)
    ).astype(BF)
    head_normed = head_normed.reshape(seq_rows, heads_local * HD)
    flat_ids = expert_ids.reshape(-1)
    n = flat_ids.shape[0]
    at = jnp.arange(n, dtype=jnp.int32)
    same = (flat_ids[:, None] == flat_ids[None, :]) & (at[None, :] < at[:, None])
    slot_index = jnp.sum(same.astype(jnp.int32), axis=1)
    target = (flat_ids * CAP + slot_index).reshape(tok_rows, TOPK)
    chosen = target[:, :, None] == jnp.arange(slots, dtype=jnp.int32)[None, None, :]
    place = jnp.any(chosen, axis=1).astype(BF)
    gates = jnp.sum(jnp.where(chosen, expert_gates[:, :, None], 0.0), axis=1)
    gates_high = gates.astype(BF)
    gates_low = (gates - gates_high.astype(F32)).astype(BF)
    gates_two = jnp.concatenate([gates_high, gates_low], axis=0)
    partial = jnp.dot(head_normed, full_out, preferred_element_type=F32)
    attention = sum_heads(partial, z, c)
    residual_float = (stream.astype(F32) + attention).astype(BF).astype(F32)
    mean_square = jnp.mean(residual_float * residual_float, axis=-1, keepdims=True)
    normed = (residual_float * lax.rsqrt(mean_square + 1e-06) * model_gain).astype(BF)
    outgoing = jnp.einsum("ts,td->sd", place, normed, preferred_element_type=F32).astype(BF)
    lanes = 128
    message = outgoing.reshape(experts, CAP * D // lanes, lanes)
    arrived = lax.all_to_all(message, ("seq", "head"), split_axis=0, concat_axis=0, tiled=True)
    slot_rows = arrived.reshape(slots, D)
    scale_row = weight_scales[0]
    gate_part = jnp.dot(slot_rows, gate_weight[0], preferred_element_type=F32) * scale_row[0]
    up_part = jnp.dot(slot_rows, up_weight[0], preferred_element_type=F32) * scale_row[1]
    act = (jax.nn.silu(gate_part) * up_part).astype(BF)
    produced = jnp.dot(act, down_weight[0], preferred_element_type=F32) * scale_row[2]
    message = produced.astype(BF).reshape(experts, CAP * D // lanes, lanes)
    results = lax.all_to_all(message, ("seq", "head"), split_axis=0, concat_axis=0, tiled=True)
    results = results.reshape(slots, D)
    both = jnp.dot(gates_two, results, preferred_element_type=F32)
    expert_mix = both[:tok_rows] + both[tok_rows:]
    return (residual_float + expert_mix).astype(BF)


def solution(mesh):
    token = P(("seq", "head"), None)
    expert = P(("seq", "head"), None, None)
    return jax.shard_map(
        body,
        mesh=mesh,
        in_specs=(
            P("seq", "head"),
            P("seq", "head"),
            P("seq", "head"),
            P("head"),
            P("head", "seq"),
            token,
            P(),
            token,
            token,
            expert,
            expert,
            expert,
            token,
        ),
        out_specs=token,
        check_vma=False,
    )
```

profile of v0, /device:TPU:1, one launch (start us, length us, event | category | flops | bytes accessed | tf_op | source)
XLA Modules:
  0.0 246.5 jit_solution(13957495050865137763)
XLA Ops:
  8.6 2.2 collective-permute-start
  10.8 2.6 %collective-permute-start.1 = (bf16[4,128,128]{2,1,0:T(8,128)(2,1)S(1)}, bf16[4,128,128]{2,1,0:T(8,128)(2,1)S(1)}, u32[]{:S(2)}, u32[]{:S(2)}) collective-permute-start(bf16[4,128,128]{2,1,0:T(8,128)(2,1)S(1)} %get-tuple-element.17), channel_id=1, source_target_pairs={{0,16},{8,24},{16,0},{24,8},{32,48},{40,56},{48,32},{56,40},{64,80... | collective-permute-start | bytes 393224 | tf_op jit(solution)/shard_map/ppermute | solution.py:22
  15.3 3.8 %collective-permute-done.1 = bf16[4,128,128]{2,1,0:T(8,128)(2,1)S(1)} collective-permute-done((bf16[4,128,128]{2,1,0:T(8,128)(2,1)S(1)}, bf16[4,128,128]{2,1,0:T(8,128)(2,1)S(1)}, u32[]{:S(2)}, u32[]{:S(2)}) %collective-permute-start.1) | collective-permute-done | bytes 131104 | tf_op jit(solution)/shard_map/ppermute | solution.py:22
  20.5 2.5 collective-permute-start.4
  24.3 3.8 %collective-permute-done.4 = bf16[4,128,128]{2,1,0:T(8,128)(2,1)S(1)} collective-permute-done((bf16[4,128,128]{2,1,0:T(8,128)(2,1)S(1)}, bf16[4,128,128]{2,1,0:T(8,128)(2,1)S(1)}, u32[]{:S(2)}, u32[]{:S(2)}) %collective-permute-start.4) | collective-permute-done | bytes 131104 | tf_op jit(solution)/shard_map/ppermute | solution.py:17
  32.1 39.6 %all-gather.2.cloned.1.call-done = bf16[512,4096]{1,0:T(8,128)(2,1)} async-done(((bf16[512,256]{1,0:T(8,128)(2,1)}), bf16[512,4096]{1,0:T(8,128)(2,1)}) %all-gather.2.cloned.1.call-update) | async-done | bytes 4194320 | tf_op jit(solution)/shard_map/all_gather | solution.py:87
  71.7 3.4 %fusion.8 = f32[4,2,32,4096]{3,2,1,0:T(8,128)S(1)} fusion(bf16[4,2,32,512]{3,2,1,0:T(8,128)(2,1)S(1)} %dot_general.36, bf16[512,4096]{1,0:T(8,128)(2,1)} %all-gather.2.cloned.1.call-done), kind=kOutput, calls=%fused_computation.8 | convolution fusion | flops 1073741824 | bytes 8650752 | tf_op jit(solution)/shard_map/dot_general | solution.py:118
  75.1 1.9 copy-done.1
  79.3 1.8 collective-permute-done.6
  81.2 2.6 %fusion.83 = (bf16[4,32,4096]{2,1,0:T(8,128)(2,1)S(1)}, f32[4,32,4096]{2,1,0:T(8,128)S(1)}) fusion(bf16[4,32,4096]{2,1,0:T(8,128)(2,1)S(1)} %collective-permute-done.6, f32[4,2,32,4096]{3,2,1,0:T(8,128)} %copy-done.1, pred[]{:T(512)S(6)} %eq.37), kind=kLoop, calls=%fused_computation.97 | loop fusion | flops 2097152 | bytes 8388609 | tf_op jit(solution)/shard_map/convert_element_type | solution.py:56
  85.2 2.6 %collective-permute-start.8 = (bf16[32,4096]{1,0:T(8,128)(2,1)S(1)}, bf16[32,4096]{1,0:T(8,128)(2,1)S(1)}, u32[]{:S(2)}, u32[]{:S(2)}) collective-permute-start(bf16[32,4096]{1,0:T(8,128)(2,1)S(1)} %get-tuple-element.13), channel_id=1, source_target_pairs={{0,4},{1,5},{2,6},{3,7},{4,0},{5,1},{6,2},{7,3},{8,12},{9,13},{10,... | collective-permute-start | bytes 786440 | tf_op jit(solution)/shard_map/ppermute | solution.py:27
  89.1 3.6 %collective-permute-done.7 = bf16[32,4096]{1,0:T(8,128)(2,1)S(1)} collective-permute-done((bf16[32,4096]{1,0:T(8,128)(2,1)S(1)}, bf16[32,4096]{1,0:T(8,128)(2,1)S(1)}, u32[]{:S(2)}, u32[]{:S(2)}) %collective-permute-start.7) | collective-permute-done | bytes 262176 | tf_op jit(solution)/shard_map/ppermute | solution.py:27
  92.6 6.8 %collective-permute-done.8 = bf16[32,4096]{1,0:T(8,128)(2,1)S(1)} collective-permute-done((bf16[32,4096]{1,0:T(8,128)(2,1)S(1)}, bf16[32,4096]{1,0:T(8,128)(2,1)S(1)}, u32[]{:S(2)}, u32[]{:S(2)}) %collective-permute-start.8) | collective-permute-done | bytes 262176 | tf_op jit(solution)/shard_map/ppermute | solution.py:27
  101.5 3.4 %reshape.74 = bf16[128,96,128]{2,1,0:T(8,128)(2,1)} reshape(bf16[384,4096]{1,0:T(8,128)(2,1)S(1)} %convolution_convert_fusion) | data formatting | bytes 6291456 | tf_op jit(solution)/shard_map/reshape | solution.py:125
  104.9 7.7 %all-to-all-start = ((bf16[128,96,128]{2,1,0:T(8,128)(2,1)}), bf16[128,96,128]{2,1,0:T(8,128)(2,1)S(1)}, u32[]{:S(2)}, u32[]{:S(2)}) async-start(bf16[128,96,128]{2,1,0:T(8,128)(2,1)} %reshape.74), calls=%async_computation | async-start | bytes 6291456 | tf_op jit(solution)/shard_map/all_to_all | solution.py:126
  113.3 41.2 %all-to-all-done = bf16[128,96,128]{2,1,0:T(8,128)(2,1)S(1)} async-done(((bf16[128,96,128]{2,1,0:T(8,128)(2,1)}), bf16[128,96,128]{2,1,0:T(8,128)(2,1)S(1)}, u32[]{:S(2)}, u32[]{:S(2)}) %all-to-all-start) | async-done | bytes 3145760 | tf_op jit(solution)/shard_map/all_to_all | solution.py:126
  154.4 3.3 %reshape.75 = bf16[384,4096]{1,0:T(8,128)(2,1)} reshape(bf16[128,96,128]{2,1,0:T(8,128)(2,1)S(1)} %all-to-all-done) | data formatting | bytes 6291456 | tf_op jit(solution)/shard_map/reshape | solution.py:127
  157.8 8.1 %fusion.12 = f32[384,768]{1,0:T(8,128)} fusion(bf16[384,4096]{1,0:T(8,128)(2,1)} %reshape.75, bf16[1,4096,768]{2,1,0:T(8,128)(2,1)} %param.22, f32[]{:T(128)} %bitcast.15), kind=kOutput, calls=%fused_computation.14 | convolution fusion | flops 2416214016 | bytes 10616836 | tf_op jit(solution)/shard_map/dot_general | solution.py:129
  165.9 14.5 %multiply_convert_fusion = bf16[384,4096]{1,0:T(8,128)(2,1)} fusion(bf16[1,768,4096]{2,1,0:T(8,128)(2,1)} %param.24, f32[]{:T(128)} %bitcast.19, bf16[384,4096]{1,0:T(8,128)(2,1)S(1)} %copy-done.2, bf16[1,4096,768]{2,1,0:T(8,128)(2,1)} %param.23, f32[384,768]{1,0:T(8,128)} %fusion.12, f32[]{:T(128)} %bitcast.17), kind=kOutput, calls=%fused_computation.6 | convolution fusion | flops 4837048320 | bytes 20054024 | tf_op jit(solution)/shard_map/dot_general | solution.py:132
  180.4 5.9 %reshape.76 = bf16[128,96,128]{2,1,0:T(8,128)(2,1)} reshape(bf16[384,4096]{1,0:T(8,128)(2,1)} %multiply_convert_fusion) | data formatting | bytes 6291456 | tf_op jit(solution)/shard_map/reshape | solution.py:133
  186.3 4.7 %all-to-all-start.1 = ((bf16[128,96,128]{2,1,0:T(8,128)(2,1)}), bf16[128,96,128]{2,1,0:T(8,128)(2,1)S(1)}, u32[]{:S(2)}, u32[]{:S(2)}) async-start(bf16[128,96,128]{2,1,0:T(8,128)(2,1)} %reshape.76), calls=%async_computation.1 | async-start | bytes 6291456 | tf_op jit(solution)/shard_map/all_to_all | solution.py:134
  191.3 41.7 %all-to-all-done.1 = bf16[128,96,128]{2,1,0:T(8,128)(2,1)S(1)} async-done(((bf16[128,96,128]{2,1,0:T(8,128)(2,1)}), bf16[128,96,128]{2,1,0:T(8,128)(2,1)S(1)}, u32[]{:S(2)}, u32[]{:S(2)}) %all-to-all-start.1) | async-done | bytes 3145760 | tf_op jit(solution)/shard_map/all_to_all | solution.py:134
  233.0 3.3 %reshape.77 = bf16[384,4096]{1,0:T(8,128)(2,1)} reshape(bf16[128,96,128]{2,1,0:T(8,128)(2,1)S(1)} %all-to-all-done.1) | data formatting | bytes 6291456 | tf_op jit(solution)/shard_map/reshape | solution.py:135
  236.3 2.6 %fusion.74 = f32[64,4096]{1,0:T(8,128)S(1)} fusion(bf16[384,4096]{1,0:T(8,128)(2,1)} %reshape.77, bf16[32,384]{1,0:T(8,128)(2,1)S(1)} %get-tuple-element.5, bf16[32,384]{1,0:T(8,128)(2,1)S(1)} %get-tuple-element.6), kind=kOutput, calls=%fused_computation.85 | convolution fusion | flops 201424896 | bytes 4243456 | tf_op jit(solution)/shard_map/dot_general | solution.py:136
  (62 shorter events, 19.2 us)
Async XLA Ops:
  6.5 1.8 copy-start
  6.5 24.6 %copy-start.11 = (bf16[256,512]{1,0:T(8,128)(2,1)S(1)}, bf16[256,512]{1,0:T(8,128)(2,1)}, u32[]{:S(2)}) copy-start(bf16[256,512]{1,0:T(8,128)(2,1)} %param.13) | copy-start | bytes 786436
  6.5 65.1 %all-gather.2.cloned.1.call-start = ((), (), s32[]{:S(2)}) async-start(), calls=%async_computation.2 | async-start | bytes 4456448 | tf_op jit(solution)/shard_map/all_gather | solution.py:87
  7.3 24.4 %copy-start.10 = (f32[512]{0:T(512)S(1)}, f32[512]{0:T(512)}, u32[]{:S(2)}) copy-start(f32[512]{0:T(512)} %param.16) | copy-start | bytes 6148
  8.6 6.7 %collective-permute-start = (bf16[4,128,128]{2,1,0:T(8,128)(2,1)S(1)}, bf16[4,128,128]{2,1,0:T(8,128)(2,1)S(1)}, u32[]{:S(2)}, u32[]{:S(2)}) collective-permute-start(bf16[4,128,128]{2,1,0:T(8,128)(2,1)S(1)} %get-tuple-element.17), channel_id=1, source_target_pairs={{0,8},{8,16},{16,24},{24,0},{32,40},{40,48},{48,56},{56,32},{64,72... | collective-permute-start | bytes 393224 | tf_op jit(solution)/shard_map/ppermute | solution.py:22
  10.8 8.3 %collective-permute-start.1 = (bf16[4,128,128]{2,1,0:T(8,128)(2,1)S(1)}, bf16[4,128,128]{2,1,0:T(8,128)(2,1)S(1)}, u32[]{:S(2)}, u32[]{:S(2)}) collective-permute-start(bf16[4,128,128]{2,1,0:T(8,128)(2,1)S(1)} %get-tuple-element.17), channel_id=1, source_target_pairs={{0,16},{8,24},{16,0},{24,8},{32,48},{40,56},{48,32},{56,40},{64,80... | collective-permute-start | bytes 393224 | tf_op jit(solution)/shard_map/ppermute | solution.py:22
  13.4 5.7 %collective-permute-start.2 = (bf16[4,128,128]{2,1,0:T(8,128)(2,1)S(1)}, bf16[4,128,128]{2,1,0:T(8,128)(2,1)S(1)}, u32[]{:S(2)}, u32[]{:S(2)}) collective-permute-start(bf16[4,128,128]{2,1,0:T(8,128)(2,1)S(1)} %get-tuple-element.17), channel_id=1, source_target_pairs={{0,24},{8,0},{16,8},{24,16},{32,56},{40,32},{48,40},{56,48},{64,88... | collective-permute-start | bytes 393224 | tf_op jit(solution)/shard_map/ppermute | solution.py:22
  19.2 5.1 %collective-permute-start.3 = (bf16[4,128,128]{2,1,0:T(8,128)(2,1)S(1)}, bf16[4,128,128]{2,1,0:T(8,128)(2,1)S(1)}, u32[]{:S(2)}, u32[]{:S(2)}) collective-permute-start(bf16[4,128,128]{2,1,0:T(8,128)(2,1)S(1)} %fusion.50), channel_id=1, source_target_pairs={{0,32},{8,40},{16,48},{24,56},{32,64},{40,72},{48,80},{56,88},{64,... | collective-permute-start | bytes 393224 | tf_op jit(solution)/shard_map/ppermute | solution.py:17
  20.5 7.6 %collective-permute-start.4 = (bf16[4,128,128]{2,1,0:T(8,128)(2,1)S(1)}, bf16[4,128,128]{2,1,0:T(8,128)(2,1)S(1)}, u32[]{:S(2)}, u32[]{:S(2)}) collective-permute-start(bf16[4,128,128]{2,1,0:T(8,128)(2,1)S(1)} %fusion.50), channel_id=1, source_target_pairs={{0,64},{8,72},{16,80},{24,88},{32,96},{40,104},{48,112},{56,120},{... | collective-permute-start | bytes 393224 | tf_op jit(solution)/shard_map/ppermute | solution.py:17
  22.9 6.9 %collective-permute-start.5 = (bf16[4,128,128]{2,1,0:T(8,128)(2,1)S(1)}, bf16[4,128,128]{2,1,0:T(8,128)(2,1)S(1)}, u32[]{:S(2)}, u32[]{:S(2)}) collective-permute-start(bf16[4,128,128]{2,1,0:T(8,128)(2,1)S(1)} %fusion.50), channel_id=1, source_target_pairs={{0,96},{8,104},{16,112},{24,120},{32,0},{40,8},{48,16},{56,24},{64... | collective-permute-start | bytes 393224 | tf_op jit(solution)/shard_map/ppermute | solution.py:17
  75.1 1.9 copy-start.1
  77.1 1.8 copy-start.8
  77.3 3.9 %collective-permute-start.6 = (bf16[4,32,4096]{2,1,0:T(8,128)(2,1)S(1)}, bf16[4,32,4096]{2,1,0:T(8,128)(2,1)S(1)}, u32[]{:S(2)}, u32[]{:S(2)}) collective-permute-start(bf16[4,32,4096]{2,1,0:T(8,128)(2,1)S(1)} %fusion.28), channel_id=1, source_target_pairs={{0,1},{1,0},{2,3},{3,2},{4,5},{5,4},{6,7},{7,6},{8,9},{9,8},{10,11... | collective-permute-start | bytes 3145736 | tf_op jit(solution)/shard_map/ppermute | solution.py:32
  79.3 20.1 %copy-start.5 = (bf16[32,4096]{1,0:T(8,128)(2,1)S(1)}, bf16[32,4096]{1,0:T(8,128)(2,1)}, u32[]{:S(2)}) copy-start(bf16[32,4096]{1,0:T(8,128)(2,1)} %param.18) | copy-start | bytes 786436
  83.8 16.7 %copy-start.6 = (f32[4096]{0:T(1024)S(1)}, f32[4096]{0:T(1024)}, u32[]{:S(2)}) copy-start(f32[4096]{0:T(1024)} %param.19) | copy-start | bytes 49156
  83.8 8.8 %collective-permute-start.7 = (bf16[32,4096]{1,0:T(8,128)(2,1)S(1)}, bf16[32,4096]{1,0:T(8,128)(2,1)S(1)}, u32[]{:S(2)}, u32[]{:S(2)}) collective-permute-start(bf16[32,4096]{1,0:T(8,128)(2,1)S(1)} %get-tuple-element.11), channel_id=1, source_target_pairs={{0,2},{1,3},{2,4},{3,5},{4,6},{5,7},{6,0},{7,1},{8,10},{9,11},{10,... | collective-permute-start | bytes 786440 | tf_op jit(solution)/shard_map/ppermute | solution.py:27
  85.2 14.2 %collective-permute-start.8 = (bf16[32,4096]{1,0:T(8,128)(2,1)S(1)}, bf16[32,4096]{1,0:T(8,128)(2,1)S(1)}, u32[]{:S(2)}, u32[]{:S(2)}) collective-permute-start(bf16[32,4096]{1,0:T(8,128)(2,1)S(1)} %get-tuple-element.13), channel_id=1, source_target_pairs={{0,4},{1,5},{2,6},{3,7},{4,0},{5,1},{6,2},{7,3},{8,12},{9,13},{10,... | collective-permute-start | bytes 786440 | tf_op jit(solution)/shard_map/ppermute | solution.py:27
  87.8 11.7 %collective-permute-start.9 = (bf16[32,4096]{1,0:T(8,128)(2,1)S(1)}, bf16[32,4096]{1,0:T(8,128)(2,1)S(1)}, u32[]{:S(2)}, u32[]{:S(2)}) collective-permute-start(bf16[32,4096]{1,0:T(8,128)(2,1)S(1)} %get-tuple-element.12), channel_id=1, source_target_pairs={{0,6},{1,7},{2,0},{3,1},{4,2},{5,3},{6,4},{7,5},{8,14},{9,15},{10,... | collective-permute-start | bytes 786440 | tf_op jit(solution)/shard_map/ppermute | solution.py:27
  104.9 7.7 %copy-start.7 = (f32[1,3]{1,0:T(1,128)S(1)}, f32[1,3]{1,0:T(1,128)}, u32[]{:S(2)}) copy-start(f32[1,3]{1,0:T(1,128)} %param.25) | copy-start | bytes 40
  104.9 49.5 %all-to-all-start = ((bf16[128,96,128]{2,1,0:T(8,128)(2,1)}), bf16[128,96,128]{2,1,0:T(8,128)(2,1)S(1)}, u32[]{:S(2)}, u32[]{:S(2)}) async-start(bf16[128,96,128]{2,1,0:T(8,128)(2,1)} %reshape.74), calls=%async_computation | async-start | bytes 6291456 | tf_op jit(solution)/shard_map/all_to_all | solution.py:126
  157.8 8.2 %copy-start.2 = (bf16[384,4096]{1,0:T(8,128)(2,1)S(1)}, bf16[384,4096]{1,0:T(8,128)(2,1)}, u32[]{:S(2)}) copy-start(bf16[384,4096]{1,0:T(8,128)(2,1)} %reshape.75) | copy-start | bytes 9437188
  186.3 4.7 %copy-start.9 = (f32[32,8]{0,1:T(8,128)S(1)}, f32[32,8]{0,1:T(8,128)}, u32[]{:S(2)}) copy-start(f32[32,8]{0,1:T(8,128)} %param.21) | copy-start | bytes 3076
  186.3 46.7 %all-to-all-start.1 = ((bf16[128,96,128]{2,1,0:T(8,128)(2,1)}), bf16[128,96,128]{2,1,0:T(8,128)(2,1)S(1)}, u32[]{:S(2)}, u32[]{:S(2)}) async-start(bf16[128,96,128]{2,1,0:T(8,128)(2,1)} %reshape.76), calls=%async_computation.1 | async-start | bytes 6291456 | tf_op jit(solution)/shard_map/all_to_all | solution.py:134
  236.3 2.6 %copy-start.4 = (bf16[32,4096]{1,0:T(8,128)(2,1)S(1)}, bf16[32,4096]{1,0:T(8,128)(2,1)}, u32[]{:S(2)}) copy-start(bf16[32,4096]{1,0:T(8,128)(2,1)} %copy-done.3) | copy-start | bytes 786436
  (1 other events, 0.7 us)
Sparse Core Ops, SparseCore 0:
  9.5 62.1 all-gather.1
where the time goes:
time: 247 us
  waiting for transfers between devices  146 us (59%)
  matrix products  31.8 us (13%)
  starting transfers between devices  29.7 us (12%)
  local copies, waits for them, and re-layouts  21 us (9%)
  between operations  13.6 us (6%)
  other arithmetic  4.65 us (2%)
    all_to_all x2, waiting for transfers between devices, body(): lax.all_to_all(message, ('seq', 'head'), split_axis=0, concat_axis=0, til...  82.8 us
    all_gather x1, waiting for transfers between devices, body(): full_out = lax.all_gather(out_weight, 'seq', axis=1, tiled=True)  39.6 us
    dot_general x1, matrix products, body(): jnp.dot(act, down_weight[0], preferred_element_type=F32) * scale_row[2]  14.5 us
    all_to_all x2, starting transfers between devices, body(): lax.all_to_all(message, ('seq', 'head'), split_axis=0, concat_axis=0, til...  12.4 us
    ppermute x3, waiting for transfers between devices, shift_z(): return lax.ppermute(a, 'head', pairs)  10.4 us
    dot_general x1, matrix products, body(): jnp.dot(slot_rows, gate_weight[0], preferred_element_type=F32)  8.15 us
    ppermute x3, starting transfers between devices, shift_y(): return lax.ppermute(a, 'seq', pairs)  5.88 us
    reshape x1, local copies, waits for them, and re-layouts, body(): message = produced.astype(BF).reshape(experts, CAP * D // lanes, lanes)  5.87 us
  transfers between devices with their start and end apart: 13, of which 11 were waited for; matrix products, arithmetic and copies ran while one was open for 2% of the time, Pallas kernels for 0%

commit v1 on v0

--- a/solution.py
+++ b/solution.py
@@ -84,7 +84,9 @@
     heads_local = head_gain.shape[0] // HD
     experts = lax.axis_size("seq") * lax.axis_size("head")
     slots = experts * CAP
-    full_out = lax.all_gather(out_weight, "seq", axis=1, tiled=True)
+    full_out = jnp.concatenate(
+        lax.all_to_all(jnp.stack([out_weight] * lax.axis_size("seq")), "seq", 0, 0), axis=1
+    )
     query_rows = query.reshape(seq_rows, heads_local, HD)
     key_rows = key.reshape(seq_rows, heads_local, HD)
     value_rows = value.reshape(seq_rows, heads_local, HD)

time: 247 us -> 265 us (1.073)
  local copies, waits for them, and re-layouts: 21 us -> 36.7 us
  starting transfers between devices: 29.7 us -> 45.2 us
  between operations: 13.6 us -> 0.28 us
    ppermute x3, waiting for transfers between devices: 4.64 us -> 47.6 us  [shift_y(): return lax.ppermute(a, 'seq', pairs)]
    all_gather x1 -> x0, waiting for transfers between devices: 39.6 us -> none  [body(): full_out = lax.all_gather(out_weight, 'seq', axis=1, tiled=True)]
    reshape x0 -> x2, local copies, waits for them, and re-layouts: none -> 13.9 us  [body(): jnp.concatenate(lax.all_to_all(jnp.stack([out_weight] * lax.axis_size('se...]
    all_to_all x0 -> x1, starting transfers between devices: none -> 7.77 us  [body(): lax.all_to_all(jnp.stack([out_weight] * lax.axis_size('seq')), 'seq', 0, 0)]
    ppermute x3, starting transfers between devices: 4.87 us -> 10.8 us  [shift_x(): return lax.ppermute(a, 'seq', pairs)]
    another operation x0 -> x1, local copies, waits for them, and re-layouts: none -> 3.4 us  [body(): jnp.stack([out_weight] * lax.axis_size('seq'))]
  transfers between devices with their start and end apart: 13 -> 13, of which waited for: 11 -> 8; matrix products, arithmetic and copies ran while one was open for 2% -> 1% of each run, Pallas kernels for 0% -> 0%
where the time goes in v1:
time: 265 us; the launch traced here: 264 us
  waiting for transfers between devices  146 us (55%)
  starting transfers between devices  45.2 us (17%)
  local copies, waits for them, and re-layouts  36.7 us (14%)
  matrix products  30.8 us (12%)
  other arithmetic  4.65 us (2%)
    all_to_all x2, waiting for transfers between devices, body(): lax.all_to_all(message, ('seq', 'head'), split_axis=0, concat_axis=0, til...  82.9 us
    ppermute x3, waiting for transfers between devices, shift_y(): return lax.ppermute(a, 'seq', pairs)  47.6 us
    dot_general x1, matrix products, body(): jnp.dot(act, down_weight[0], preferred_element_type=F32) * scale_row[2]  14.4 us
    reshape x2, local copies, waits for them, and re-layouts, body(): jnp.concatenate(lax.all_to_all(jnp.stack([out_weight] * lax.axis_size('se...  13.9 us
    all_to_all x2, starting transfers between devices, body(): lax.all_to_all(message, ('seq', 'head'), split_axis=0, concat_axis=0, til...  12.8 us
    ppermute x3, starting transfers between devices, shift_x(): return lax.ppermute(a, 'seq', pairs)  10.8 us
    ppermute x3, waiting for transfers between devices, shift_z(): return lax.ppermute(a, 'head', pairs)  10.7 us
    dot_general x1, matrix products, body(): jnp.dot(slot_rows, gate_weight[0], preferred_element_type=F32)  8.28 us
  transfers between devices with their start and end apart: 13, of which 8 were waited for; matrix products, arithmetic and copies ran while one was open for 1% of the time, Pallas kernels for 0%

profile of v1, /device:TPU:1, one launch (start us, length us, event | category | flops | bytes accessed | tf_op | source)
XLA Modules:
  0.0 264.0 jit_solution(18020940128387502153)
XLA Ops:
  0.0 3.4 %stack.2 = bf16[16,512,256]{2,1,0:T(8,128)(2,1)} broadcast(bf16[512,256]{1,0:T(8,128)(2,1)} %param.17), dimensions={1,2} | broadcast | bytes 4456448 | tf_op jit(solution)/shard_map/stack | solution.py:88
  3.4 7.8 %all-to-all-start = ((bf16[16,512,256]{2,1,0:T(8,128)(2,1)}), bf16[16,512,256]{2,1,0:T(8,128)(2,1)}, u32[]{:S(2)}, u32[]{:S(2)}) async-start(bf16[16,512,256]{2,1,0:T(8,128)(2,1)} %stack.2), calls=%async_computation | async-start | bytes 8388608 | tf_op jit(solution)/shard_map/all_to_all | solution.py:88
  16.5 47.5 %collective-permute-done = bf16[4,128,128]{2,1,0:T(8,128)(2,1)S(1)} collective-permute-done((bf16[4,128,128]{2,1,0:T(8,128)(2,1)S(1)}, bf16[4,128,128]{2,1,0:T(8,128)(2,1)S(1)}, u32[]{:S(2)}, u32[]{:S(2)}) %collective-permute-start) | collective-permute-done | bytes 131104 | tf_op jit(solution)/shard_map/ppermute | solution.py:22
  64.2 8.4 %collective-permute-start.3 = (bf16[4,128,128]{2,1,0:T(8,128)(2,1)S(1)}, bf16[4,128,128]{2,1,0:T(8,128)(2,1)S(1)}, u32[]{:S(2)}, u32[]{:S(2)}) collective-permute-start(bf16[4,128,128]{2,1,0:T(8,128)(2,1)S(1)} %fusion.50), channel_id=1, source_target_pairs={{0,32},{8,40},{16,48},{24,56},{32,64},{40,72},{48,80},{56,88},{64,... | collective-permute-start | bytes 393224 | tf_op jit(solution)/shard_map/ppermute | solution.py:17
  75.3 3.1 %collective-permute-done.4 = bf16[4,128,128]{2,1,0:T(8,128)(2,1)S(1)} collective-permute-done((bf16[4,128,128]{2,1,0:T(8,128)(2,1)S(1)}, bf16[4,128,128]{2,1,0:T(8,128)(2,1)S(1)}, u32[]{:S(2)}, u32[]{:S(2)}) %collective-permute-start.4) | collective-permute-done | bytes 131104 | tf_op jit(solution)/shard_map/ppermute | solution.py:17
  79.8 6.6 %copy.63 = bf16[512,16,256]{2,1,0:T(8,128)(2,1)} copy(bf16[512,16,256]{2,0,1:T(8,128)(2,1)} %bitcast.3) | data formatting | bytes 8388608 | tf_op jit(solution)/shard_map/reshape | solution.py:87
  86.3 7.4 %reshape.88 = bf16[512,4096,1,1]{1,0,2,3:T(8,128)(2,1)} reshape(bf16[512,16,256]{2,1,0:T(8,128)(2,1)} %copy.63) | data formatting | bytes 8388608 | tf_op jit(solution)/shard_map/reshape | solution.py:87
  93.7 3.4 %fusion.8 = f32[4,2,32,4096]{3,2,1,0:T(8,128)S(1)} fusion(bf16[4,2,32,512]{3,2,1,0:T(8,128)(2,1)S(1)} %dot_general.36, bf16[512,4096,1,1]{1,0,2,3:T(8,128)(2,1)} %reshape.88), kind=kOutput, calls=%fused_computation.8 | convolution fusion | flops 1073741824 | bytes 8650752 | tf_op jit(solution)/shard_map/dot_general | solution.py:120
  99.3 3.1 %collective-permute-start.6 = (bf16[4,32,4096]{2,1,0:T(8,128)(2,1)S(1)}, bf16[4,32,4096]{2,1,0:T(8,128)(2,1)S(1)}, u32[]{:S(2)}, u32[]{:S(2)}) collective-permute-start(bf16[4,32,4096]{2,1,0:T(8,128)(2,1)S(1)} %fusion.28), channel_id=1, source_target_pairs={{0,1},{1,0},{2,3},{3,2},{4,5},{5,4},{6,7},{7,6},{8,9},{9,8},{10,11... | collective-permute-start | bytes 3145736 | tf_op jit(solution)/shard_map/ppermute | solution.py:32
  104.6 2.6 fusion.83
  109.0 3.3 %collective-permute-start.8 = (bf16[32,4096]{1,0:T(8,128)(2,1)S(1)}, bf16[32,4096]{1,0:T(8,128)(2,1)S(1)}, u32[]{:S(2)}, u32[]{:S(2)}) collective-permute-start(bf16[32,4096]{1,0:T(8,128)(2,1)S(1)} %get-tuple-element.13), channel_id=1, source_target_pairs={{0,4},{1,5},{2,6},{3,7},{4,0},{5,1},{6,2},{7,3},{8,12},{9,13},{10,... | collective-permute-start | bytes 786440 | tf_op jit(solution)/shard_map/ppermute | solution.py:27
  113.2 4.3 %collective-permute-done.7 = bf16[32,4096]{1,0:T(8,128)(2,1)S(1)} collective-permute-done((bf16[32,4096]{1,0:T(8,128)(2,1)S(1)}, bf16[32,4096]{1,0:T(8,128)(2,1)S(1)}, u32[]{:S(2)}, u32[]{:S(2)}) %collective-permute-start.7) | collective-permute-done | bytes 262176 | tf_op jit(solution)/shard_map/ppermute | solution.py:27
  117.5 6.5 %collective-permute-done.8 = bf16[32,4096]{1,0:T(8,128)(2,1)S(1)} collective-permute-done((bf16[32,4096]{1,0:T(8,128)(2,1)S(1)}, bf16[32,4096]{1,0:T(8,128)(2,1)S(1)}, u32[]{:S(2)}, u32[]{:S(2)}) %collective-permute-start.8) | collective-permute-done | bytes 262176 | tf_op jit(solution)/shard_map/ppermute | solution.py:27
  125.3 3.4 %reshape.84 = bf16[128,96,128]{2,1,0:T(8,128)(2,1)} reshape(bf16[384,4096]{1,0:T(8,128)(2,1)S(1)} %convolution_convert_fusion) | data formatting | bytes 6291456 | tf_op jit(solution)/shard_map/reshape | solution.py:127
  128.8 8.1 %all-to-all-start.1 = ((bf16[128,96,128]{2,1,0:T(8,128)(2,1)}), bf16[128,96,128]{2,1,0:T(8,128)(2,1)S(1)}, u32[]{:S(2)}, u32[]{:S(2)}) async-start(bf16[128,96,128]{2,1,0:T(8,128)(2,1)} %reshape.84), calls=%async_computation.1 | async-start | bytes 6291456 | tf_op jit(solution)/shard_map/all_to_all | solution.py:128
  137.5 41.2 %all-to-all-done.1 = bf16[128,96,128]{2,1,0:T(8,128)(2,1)S(1)} async-done(((bf16[128,96,128]{2,1,0:T(8,128)(2,1)}), bf16[128,96,128]{2,1,0:T(8,128)(2,1)S(1)}, u32[]{:S(2)}, u32[]{:S(2)}) %all-to-all-start.1) | async-done | bytes 3145760 | tf_op jit(solution)/shard_map/all_to_all | solution.py:128
  178.7 3.3 %reshape.85 = bf16[384,4096]{1,0:T(8,128)(2,1)} reshape(bf16[128,96,128]{2,1,0:T(8,128)(2,1)S(1)} %all-to-all-done.1) | data formatting | bytes 6291456 | tf_op jit(solution)/shard_map/reshape | solution.py:129
  182.1 8.3 %fusion.12 = f32[384,768]{1,0:T(8,128)} fusion(bf16[384,4096]{1,0:T(8,128)(2,1)} %reshape.85, bf16[1,4096,768]{2,1,0:T(8,128)(2,1)} %param.22, f32[]{:T(128)} %bitcast.15), kind=kOutput, calls=%fused_computation.14 | convolution fusion | flops 2416214016 | bytes 10616836 | tf_op jit(solution)/shard_map/dot_general | solution.py:131
  190.4 14.4 %multiply_convert_fusion = bf16[384,4096]{1,0:T(8,128)(2,1)} fusion(bf16[1,768,4096]{2,1,0:T(8,128)(2,1)} %param.24, f32[]{:T(128)} %bitcast.19, bf16[384,4096]{1,0:T(8,128)(2,1)S(1)} %copy-done.3, bf16[1,4096,768]{2,1,0:T(8,128)(2,1)} %param.23, f32[384,768]{1,0:T(8,128)} %fusion.12, f32[]{:T(128)} %bitcast.17), kind=kOutput, calls=%fused_computation.6 | convolution fusion | flops 4837048320 | bytes 20054024 | tf_op jit(solution)/shard_map/dot_general | solution.py:134
  204.7 5.9 %reshape.86 = bf16[128,96,128]{2,1,0:T(8,128)(2,1)} reshape(bf16[384,4096]{1,0:T(8,128)(2,1)} %multiply_convert_fusion) | data formatting | bytes 6291456 | tf_op jit(solution)/shard_map/reshape | solution.py:135
  210.6 4.7 %all-to-all-start.2 = ((bf16[128,96,128]{2,1,0:T(8,128)(2,1)}), bf16[128,96,128]{2,1,0:T(8,128)(2,1)S(1)}, u32[]{:S(2)}, u32[]{:S(2)}) async-start(bf16[128,96,128]{2,1,0:T(8,128)(2,1)} %reshape.86), calls=%async_computation.2 | async-start | bytes 6291456 | tf_op jit(solution)/shard_map/all_to_all | solution.py:136
  215.6 41.7 %all-to-all-done.2 = bf16[128,96,128]{2,1,0:T(8,128)(2,1)S(1)} async-done(((bf16[128,96,128]{2,1,0:T(8,128)(2,1)}), bf16[128,96,128]{2,1,0:T(8,128)(2,1)S(1)}, u32[]{:S(2)}, u32[]{:S(2)}) %all-to-all-start.2) | async-done | bytes 3145760 | tf_op jit(solution)/shard_map/all_to_all | solution.py:136
  257.3 3.3 %reshape.87 = bf16[384,4096]{1,0:T(8,128)(2,1)} reshape(bf16[128,96,128]{2,1,0:T(8,128)(2,1)S(1)} %all-to-all-done.2) | data formatting | bytes 6291456 | tf_op jit(solution)/shard_map/reshape | solution.py:137
  260.6 2.6 fusion.74
  (68 shorter events, 19.5 us)
Async XLA Ops:
  0.0 11.3 %copy-start = (bf16[256,512]{1,0:T(8,128)(2,1)S(1)}, bf16[256,512]{1,0:T(8,128)(2,1)}, u32[]{:S(2)}) copy-start(bf16[256,512]{1,0:T(8,128)(2,1)} %param.15) | copy-start | bytes 786436
  3.4 7.8 %copy-start.7 = (bf16[256,512]{1,0:T(8,128)(2,1)S(1)}, bf16[256,512]{1,0:T(8,128)(2,1)}, u32[]{:S(2)}) copy-start(bf16[256,512]{1,0:T(8,128)(2,1)} %param.14) | copy-start | bytes 786436
  3.4 75.0 %copy-start.13 = (bf16[256,512]{1,0:T(8,128)(2,1)S(1)}, bf16[256,512]{1,0:T(8,128)(2,1)}, u32[]{:S(2)}) copy-start(bf16[256,512]{1,0:T(8,128)(2,1)} %param.13) | copy-start | bytes 786436
  3.4 76.3 %all-to-all-start = ((bf16[16,512,256]{2,1,0:T(8,128)(2,1)}), bf16[16,512,256]{2,1,0:T(8,128)(2,1)}, u32[]{:S(2)}, u32[]{:S(2)}) async-start(bf16[16,512,256]{2,1,0:T(8,128)(2,1)} %stack.2), calls=%async_computation | async-start | bytes 8388608 | tf_op jit(solution)/shard_map/all_to_all | solution.py:88
  11.2 68.1 %copy-start.12 = (f32[512]{0:T(512)S(1)}, f32[512]{0:T(512)}, u32[]{:S(2)}) copy-start(f32[512]{0:T(512)} %param.16) | copy-start | bytes 6148
  11.6 52.5 %collective-permute-start = (bf16[4,128,128]{2,1,0:T(8,128)(2,1)S(1)}, bf16[4,128,128]{2,1,0:T(8,128)(2,1)S(1)}, u32[]{:S(2)}, u32[]{:S(2)}) collective-permute-start(bf16[4,128,128]{2,1,0:T(8,128)(2,1)S(1)} %get-tuple-element.17), channel_id=1, source_target_pairs={{0,8},{8,16},{16,24},{24,0},{32,40},{40,48},{48,56},{56,32},{64,72... | collective-permute-start | bytes 393224 | tf_op jit(solution)/shard_map/ppermute | solution.py:22
  13.0 51.1 %collective-permute-start.1 = (bf16[4,128,128]{2,1,0:T(8,128)(2,1)S(1)}, bf16[4,128,128]{2,1,0:T(8,128)(2,1)S(1)}, u32[]{:S(2)}, u32[]{:S(2)}) collective-permute-start(bf16[4,128,128]{2,1,0:T(8,128)(2,1)S(1)} %get-tuple-element.17), channel_id=1, source_target_pairs={{0,16},{8,24},{16,0},{24,8},{32,48},{40,56},{48,32},{56,40},{64,80... | collective-permute-start | bytes 393224 | tf_op jit(solution)/shard_map/ppermute | solution.py:22
  15.3 48.7 %collective-permute-start.2 = (bf16[4,128,128]{2,1,0:T(8,128)(2,1)S(1)}, bf16[4,128,128]{2,1,0:T(8,128)(2,1)S(1)}, u32[]{:S(2)}, u32[]{:S(2)}) collective-permute-start(bf16[4,128,128]{2,1,0:T(8,128)(2,1)S(1)} %get-tuple-element.17), channel_id=1, source_target_pairs={{0,24},{8,0},{16,8},{24,16},{32,56},{40,32},{48,40},{56,48},{64,88... | collective-permute-start | bytes 393224 | tf_op jit(solution)/shard_map/ppermute | solution.py:22
  64.2 11.1 %collective-permute-start.3 = (bf16[4,128,128]{2,1,0:T(8,128)(2,1)S(1)}, bf16[4,128,128]{2,1,0:T(8,128)(2,1)S(1)}, u32[]{:S(2)}, u32[]{:S(2)}) collective-permute-start(bf16[4,128,128]{2,1,0:T(8,128)(2,1)S(1)} %fusion.50), channel_id=1, source_target_pairs={{0,32},{8,40},{16,48},{24,56},{32,64},{40,72},{48,80},{56,88},{64,... | collective-permute-start | bytes 393224 | tf_op jit(solution)/shard_map/ppermute | solution.py:17
  72.5 5.9 %collective-permute-start.4 = (bf16[4,128,128]{2,1,0:T(8,128)(2,1)S(1)}, bf16[4,128,128]{2,1,0:T(8,128)(2,1)S(1)}, u32[]{:S(2)}, u32[]{:S(2)}) collective-permute-start(bf16[4,128,128]{2,1,0:T(8,128)(2,1)S(1)} %fusion.50), channel_id=1, source_target_pairs={{0,64},{8,72},{16,80},{24,88},{32,96},{40,104},{48,112},{56,120},{... | collective-permute-start | bytes 393224 | tf_op jit(solution)/shard_map/ppermute | solution.py:17
  72.5 5.9 %collective-permute-start.5 = (bf16[4,128,128]{2,1,0:T(8,128)(2,1)S(1)}, bf16[4,128,128]{2,1,0:T(8,128)(2,1)S(1)}, u32[]{:S(2)}, u32[]{:S(2)}) collective-permute-start(bf16[4,128,128]{2,1,0:T(8,128)(2,1)S(1)} %fusion.50), channel_id=1, source_target_pairs={{0,96},{8,104},{16,112},{24,120},{32,0},{40,8},{48,16},{56,24},{64... | collective-permute-start | bytes 393224 | tf_op jit(solution)/shard_map/ppermute | solution.py:17
  99.3 5.4 %collective-permute-start.6 = (bf16[4,32,4096]{2,1,0:T(8,128)(2,1)S(1)}, bf16[4,32,4096]{2,1,0:T(8,128)(2,1)S(1)}, u32[]{:S(2)}, u32[]{:S(2)}) collective-permute-start(bf16[4,32,4096]{2,1,0:T(8,128)(2,1)S(1)} %fusion.28), channel_id=1, source_target_pairs={{0,1},{1,0},{2,3},{3,2},{4,5},{5,4},{6,7},{7,6},{8,9},{9,8},{10,11... | collective-permute-start | bytes 3145736 | tf_op jit(solution)/shard_map/ppermute | solution.py:32
  102.8 21.2 %copy-start.6 = (bf16[32,4096]{1,0:T(8,128)(2,1)S(1)}, bf16[32,4096]{1,0:T(8,128)(2,1)}, u32[]{:S(2)}) copy-start(bf16[32,4096]{1,0:T(8,128)(2,1)} %param.18) | copy-start | bytes 786436
  107.2 17.1 %copy-start.8 = (f32[4096]{0:T(1024)S(1)}, f32[4096]{0:T(1024)}, u32[]{:S(2)}) copy-start(f32[4096]{0:T(1024)} %param.19) | copy-start | bytes 49156
  107.3 10.2 %collective-permute-start.7 = (bf16[32,4096]{1,0:T(8,128)(2,1)S(1)}, bf16[32,4096]{1,0:T(8,128)(2,1)S(1)}, u32[]{:S(2)}, u32[]{:S(2)}) collective-permute-start(bf16[32,4096]{1,0:T(8,128)(2,1)S(1)} %get-tuple-element.11), channel_id=1, source_target_pairs={{0,2},{1,3},{2,4},{3,5},{4,6},{5,7},{6,0},{7,1},{8,10},{9,11},{10,... | collective-permute-start | bytes 786440 | tf_op jit(solution)/shard_map/ppermute | solution.py:27
  109.0 15.0 %collective-permute-start.8 = (bf16[32,4096]{1,0:T(8,128)(2,1)S(1)}, bf16[32,4096]{1,0:T(8,128)(2,1)S(1)}, u32[]{:S(2)}, u32[]{:S(2)}) collective-permute-start(bf16[32,4096]{1,0:T(8,128)(2,1)S(1)} %get-tuple-element.13), channel_id=1, source_target_pairs={{0,4},{1,5},{2,6},{3,7},{4,0},{5,1},{6,2},{7,3},{8,12},{9,13},{10,... | collective-permute-start | bytes 786440 | tf_op jit(solution)/shard_map/ppermute | solution.py:27
  112.3 11.7 %collective-permute-start.9 = (bf16[32,4096]{1,0:T(8,128)(2,1)S(1)}, bf16[32,4096]{1,0:T(8,128)(2,1)S(1)}, u32[]{:S(2)}, u32[]{:S(2)}) collective-permute-start(bf16[32,4096]{1,0:T(8,128)(2,1)S(1)} %get-tuple-element.12), channel_id=1, source_target_pairs={{0,6},{1,7},{2,0},{3,1},{4,2},{5,3},{6,4},{7,5},{8,14},{9,15},{10,... | collective-permute-start | bytes 786440 | tf_op jit(solution)/shard_map/ppermute | solution.py:27
  124.3 4.5 %copy-start.4 = (bf16[32,4096]{1,0:T(8,128)(2,1)}, bf16[32,4096]{1,0:T(8,128)(2,1)S(1)}, u32[]{:S(2)}) copy-start(bf16[32,4096]{1,0:T(8,128)(2,1)S(1)} %get-tuple-element.8) | copy-start | bytes 786436
  128.8 8.1 %copy-start.9 = (f32[1,3]{1,0:T(1,128)S(1)}, f32[1,3]{1,0:T(1,128)}, u32[]{:S(2)}) copy-start(f32[1,3]{1,0:T(1,128)} %param.25) | copy-start | bytes 40
  128.8 50.0 %all-to-all-start.1 = ((bf16[128,96,128]{2,1,0:T(8,128)(2,1)}), bf16[128,96,128]{2,1,0:T(8,128)(2,1)S(1)}, u32[]{:S(2)}, u32[]{:S(2)}) async-start(bf16[128,96,128]{2,1,0:T(8,128)(2,1)} %reshape.84), calls=%async_computation.1 | async-start | bytes 6291456 | tf_op jit(solution)/shard_map/all_to_all | solution.py:128
  182.1 8.3 %copy-start.3 = (bf16[384,4096]{1,0:T(8,128)(2,1)S(1)}, bf16[384,4096]{1,0:T(8,128)(2,1)}, u32[]{:S(2)}) copy-start(bf16[384,4096]{1,0:T(8,128)(2,1)} %reshape.85) | copy-start | bytes 9437188
  210.6 4.7 %copy-start.11 = (f32[32,8]{0,1:T(8,128)S(1)}, f32[32,8]{0,1:T(8,128)}, u32[]{:S(2)}) copy-start(f32[32,8]{0,1:T(8,128)} %param.21) | copy-start | bytes 3076
  210.6 46.7 %all-to-all-start.2 = ((bf16[128,96,128]{2,1,0:T(8,128)(2,1)}), bf16[128,96,128]{2,1,0:T(8,128)(2,1)S(1)}, u32[]{:S(2)}, u32[]{:S(2)}) async-start(bf16[128,96,128]{2,1,0:T(8,128)(2,1)} %reshape.86), calls=%async_computation.2 | async-start | bytes 6291456 | tf_op jit(solution)/shard_map/all_to_all | solution.py:136
  257.3 6.7 %copy-start.1 = (bf16[256,512]{1,0:T(8,128)(2,1)S(1)}, bf16[256,512]{1,0:T(8,128)(2,1)}, u32[]{:S(2)}) copy-start(bf16[256,512]{1,0:T(8,128)(2,1)} %param.15) | copy-start | bytes 786436
  (3 other events, 7.8 us)
